TPU v7x, 256 devices: a whole 4x4x8 slice. The times are simulated.
256 devices in a mesh: fsdp: 128 (over y, x, z), rep: 2 (over core).
Axes of the slice: x: 4, y: 4, z: 8, core: 2. Of those that a mesh axis runs over, the one named last changes fastest.
Arguments:
- gradient: bfloat16 [2, 8, 4096, 4096], P('rep', None, 'fsdp'), may hold values from -80 to 80
- old_stats: float32 [2, 512, 512, 512], P('rep', 'fsdp'), may hold values from -1 to 8192, as said below
- owner_table: int32 [128, 4], replicated, may hold values from 0 to 511, as said below
Outputs:
- update: bfloat16 [8, 4096, 4096], P(None, 'fsdp')
- new_stats: float32 [2, 512, 512, 512], P('rep', 'fsdp')
Inputs may be any that keep to these rules, and one draw needn't show every extreme that they name: Every block number appears exactly once. The four entries of one row of owner_table name blocks of four different row groups ((b // 8) % 8). Each old_stats[r, s] is symmetric positive definite.
All inputs are finite; a program needn't handle non-finite values.
Results may differ from a plain program's by a relative error of at most 0.0078.
Values may be sent and summed in bfloat16 or wider, within the bound.
A program may use at most 128 MiB of HBM per device.

v0:
```python
import functools

import jax
import jax.numpy as jnp
from jax import lax
from jax.experimental import pallas as pl
from jax.experimental.pallas import tpu as pltpu
from jax.sharding import PartitionSpec as P

DECAY_RATE = 0.95
EPSILON = 1e-06
MESH = pl.DeviceIdType.MESH
F32 = jnp.float32
BF16 = jnp.bfloat16
VMEM_BYTES = 44 * 1024 * 1024

DEPTH = 8
GROUP_ROW, SLOT_ROW = 8, 16
AHEAD = 3
SPLIT = 2

COEF = tuple(
    v / 4096.0 for v in (6400.0, -4405.0, 3125.0, -1250.0, 250.0, -25.0, 1.0)
)


def steps_of(depth):
    pairs = [[low, depth - low] for low in range(depth // 2 - 1, 0, -1)]
    return [[depth // 2]] + pairs + [[0]]


class Plan:
    def __init__(self, fsdp, matrices, slab, model, slots, block):
        self.fsdp, self.matrices, self.slab, self.model = fsdp, matrices, slab, model
        self.slots, self.block = slots, block
        self.depth = DEPTH
        self.lines = fsdp // self.depth
        self.columns = model // block
        self.span = block // slab
        self.groups = fsdp // self.span
        self.tall = self.span // self.depth
        self.half = slab // 2
        self.out_steps = steps_of(self.depth)
        self.back_steps = [list(reversed(pair)) for pair in reversed(self.out_steps)]
        self.pairs = len(self.out_steps)
        self.wide = block // SPLIT
        self.land_row = SLOT_ROW + self.groups
        self.matrix_row = self.land_row + matrices * self.columns
        self.table_rows = -(-(self.matrix_row + slots) // 8) * 8
        self.start = [self.lines * sum(map(len, self.back_steps[:a])) for a in range(self.pairs)]


def dot(a, b, dims=((1,), (0,))):
    return lax.dot_general(a, b, (dims, ((), ())), preferred_element_type=F32)


def fold(rows):
    line = jnp.sum(rows, axis=0, keepdims=True)
    total = line[:, :128]
    for at in range(128, line.shape[1], 128):
        total = total + line[:, at : at + 128]
    return total


def kernel(p, owners, grad, old, upd, new, *scratch):
    (mine, theirs, gsum, send_a, land_a, send_b, blocks, eye, root, other, half_out) = scratch[:11]
    (land_c, send_d, land_d, sums, scales, sums_z, sums_l, sums_c, draft, tab, stat, made, listed, whole, land_e) = scratch[11:26]
    (load_g, load_o, save_n, save_u, pair_s, pair_r, a_s, a_r, b_s, b_r) = scratch[26:36]
    (x_s, x_r, root_s, root_r, c_s, c_r, d_s, d_r, y_s, y_r) = scratch[36:46]
    (qz_s, qz_r, ql_s, ql_r, qc_s, qc_r, tab_s, list_s, p_s, p_r) = scratch[46:]

    depth, lines, slots, block = p.depth, p.lines, p.slots, p.block
    half, tall, columns, wide, pairs = p.half, p.tall, p.columns, p.wide, p.pairs
    me = lax.axis_index("fsdp")
    core = lax.axis_index("rep")
    far_core = 1 - core
    line = lax.div(me, depth)
    place = lax.rem(me, depth)
    ahead = [lax.rem(place + k, depth) for k in range(depth)]
    behind = [lax.rem(place + depth - k, depth) for k in range(depth)]
    partner = (me, far_core)

    def at(other_line, other_place):
        return (other_line * depth + other_place, core)

    def remote(src, dst, send, recv, device):
        return pltpu.make_async_remote_copy(
            src_ref=src, dst_ref=dst, send_sem=send, recv_sem=recv,
            device_id=device, device_id_type=MESH,
        )

    def landed(ref, sem):
        pltpu.make_async_copy(ref, ref, sem).wait()

    my_rows = pl.ds(pl.multiple_of(core * half, half), half)
    far_rows = pl.ds(pl.multiple_of(far_core * half, half), half)

    barrier = pltpu.get_barrier_semaphore()

    def greet(device):
        pl.semaphore_signal(barrier, inc=1, device_id=device, device_id_type=MESH)

    greet(partner)

    @pl.loop(1, depth)
    def _(step):
        greet(at(line, lax.rem(place + step, depth)))

    @pl.loop(1, lines)
    def _(step):
        greet(at(lax.rem(line + step, lines), place))

    listing = pltpu.make_async_copy(owners, listed, list_s)
    listing.start()
    part_of = p.matrices // SPLIT

    def cut(q, c=0):
        return pl.ds(c * block + q * wide, wide)

    for q in range(SPLIT):
        for c in range(columns):
            pltpu.make_async_copy(
                grad.at[0, :, my_rows, cut(q, c)], mine.at[:, :, cut(q, c)], load_g.at[q]
            ).start()
    for j in range(slots):
        pltpu.make_async_copy(old.at[0, j], stat.at[j], load_o.at[j]).start()
    sums[...] = jnp.zeros_like(sums)
    listing.wait()
    lookup = tables(p, listed[...], me, line, place)
    for row, value in lookup:
        draft[row : row + value.shape[0], :] = value
    pltpu.make_async_copy(draft, tab, tab_s).start()
    row_id = lax.broadcasted_iota(jnp.int32, (block, block), 0)
    col_id = lax.broadcasted_iota(jnp.int32, (block, block), 1)
    eye[...] = jnp.where(row_id == col_id, COEF[0], 0.0)
    pl.semaphore_wait(barrier, depth + lines - 1)

    for q in range(SPLIT):
        for c in range(columns):
            remote(
                grad.at[0, :, far_rows, cut(q, c)], theirs.at[:, :, cut(q, c)],
                pair_s.at[q], pair_r.at[q], partner,
            ).start()

    def add(q):
        landed(mine.at[pl.ds(0, part_of)], load_g.at[q])
        landed(theirs.at[pl.ds(0, part_of)], pair_r.at[q])

        @pl.loop(0, p.matrices)
        def _(m):
            square = jnp.zeros((half, wide), F32)
            for c in range(columns):
                value = mine[m, :, cut(q, c)].astype(F32) + theirs[m, :, cut(q, c)].astype(F32)
                value = value.astype(BF16)
                gsum[q][m * columns + c] = value
                value = value.astype(F32)
                square = square + value * value
            sums[0, pl.ds(m, 1), :] = sums[0, pl.ds(m, 1), :] + fold(square)

    add(0)
    landed(tab, tab_s)

    def across(q, a, pair):
        @pl.loop(0, lines, unroll=4)
        def _(to):
            for i, k in enumerate(pair):
                send_a[q][a][to, i] = gsum[q][tab[0, to * depth + ahead[k]]]

        @pl.loop(1, lines, unroll=5)
        def _(step):
            to = lax.rem(line + step, lines)
            remote(
                send_a[q][a].at[to], land_a[q][a].at[line],
                a_s.at[q * pairs + a], a_r.at[q * pairs + a], at(to, place),
            ).start()

        for i in range(len(pair)):
            land_a[q][a][line, i] = send_a[q][a][line, i]

    def along(q, a, pair):
        landed(land_a[q][a].at[pl.ds(0, lines - 1)], a_r.at[q * pairs + a])
        for i, k in enumerate(pair):
            to = ahead[k]
            for j in range(slots):
                group = tab[GROUP_ROW + j, line * depth + to]
                for t in range(tall):
                    piece = land_a[q][a][group * tall + t, i]
                    if k:
                        send_b[q, k - 1, j, t] = piece
                    else:
                        blocks[j, t, place, core, :, cut(q)] = piece
            if k:
                remote(
                    send_b.at[q, k - 1], blocks.at[:, :, place, core, :, cut(q)],
                    b_s.at[q * depth + k], b_r.at[q * depth + k], at(line, to),
                ).start()

    out_order = [(q, a, pair) for q in range(SPLIT) for a, pair in enumerate(p.out_steps)]
    for at_step in range(len(out_order) + AHEAD):
        if at_step % pairs == min(2, pairs - 1) and at_step // pairs + 1 < SPLIT:
            add(at_step // pairs + 1)
        if at_step < len(out_order):
            across(*out_order[at_step])
        if at_step >= AHEAD:
            along(*out_order[at_step - AHEAD])

    for q, _, pair in out_order:
        for k in pair:
            rows = blocks.at[:, :, behind[k], core, :, cut(q)]
            sem = q * depth + k
            if k:
                landed(rows, b_r.at[sem])
            remote(rows, rows, x_s.at[sem], x_r.at[sem], partner).start()
    for q, _, pair in out_order:
        for k in pair:
            landed(blocks.at[:, :, behind[k], far_core, :, cut(q)], x_r.at[q * depth + k])

    share = slots // 2
    assert share == 2

    @pl.loop(0, 2)
    def _(turn):
        first = lax.rem(turn + far_core, 2) * share
        both = [first, first + 1]
        for j in both:
            landed(stat.at[j], load_o.at[j])

        def statistics(dims):
            for j in both:
                g = blocks[j].reshape(block, block)
                stat[j] = DECAY_RATE * stat[j] + dot(g, g, dims)
                pltpu.make_async_copy(stat.at[j], new.at[0, j], save_n.at[j]).start()

        pl.when(core == 0)(lambda: statistics(((1,), (1,))))
        pl.when(core == 1)(lambda: statistics(((0,), (0,))))

        def each(f, *lists):
            return [f(*values) for values in zip(*lists)]

        a = [stat[j] for j in both]
        norm2 = each(
            lambda a: jnp.sum(jnp.sum(a * a, axis=0, keepdims=True), axis=1, keepdims=True) + EPSILON, a
        )
        norm = each(jnp.sqrt, norm2)
        inverse = each(lambda n: 1.0 / n, norm)
        b1 = each(lambda a, v: (a * v).astype(BF16), a, inverse)
        m2 = each(dot, b1, b1)
        b2 = each(lambda m: m.astype(BF16), m2)
        m3 = each(dot, b1, b2)
        b3 = each(lambda m: m.astype(BF16), m3)
        c4, c5, c6 = (jnp.asarray(v, BF16) for v in COEF[4:])
        upper = each(lambda x, y, w: c4 * x + c5 * y + c6 * w, b1, b2, b3)
        high = each(dot, b3, upper)
        low = each(
            lambda a, v, m2, m3: (COEF[1] * v) * a + COEF[2] * m2 + COEF[3] * m3 + eye[...],
            a, inverse, m2, m3,
        )
        x = each(lambda h, l, n: ((h + l) * lax.rsqrt(jnp.sqrt(n))).astype(BF16), high, low, norm)
        for j, value in zip(both, x):
            root[j] = value.reshape(root.shape[1:])

        @pl.when(turn == 0)
        def _():
            for i, j in enumerate(both):
                remote(root.at[j], other.at[i], root_s.at[i], root_r.at[i], partner).start()

    def apply(j, left, right):
        g = blocks[j].reshape(block, block)
        part = dot(g, right.reshape(block, block)).astype(BF16)
        return dot(left.reshape(block, block), part).astype(BF16).reshape(whole.shape[1:])

    matrix_id = lax.broadcasted_iota(jnp.int32, sums.shape[1:], 0)
    for i in range(share):
        j = core * share + i
        landed(other.at[i], root_r.at[i])

        @pl.when(core == 0)
        def _():
            whole[i] = apply(j, root[j], other[i])

        @pl.when(core == 1)
        def _():
            whole[i] = apply(j, other[i], root[j])

        remote(whole.at[i, :, :, far_core], half_out.at[j], p_s.at[i], p_r.at[i], partner).start()
        half_out[j] = whole[i, :, :, core]
        value = whole[i].reshape(block, block).astype(F32)
        total = fold(value * value)
        sums[1] = sums[1] + jnp.where(matrix_id == tab[p.matrix_row + j, me], total, 0.0)
    for i in range(share):
        landed(half_out.at[far_core * share + i], p_r.at[i])

    sums_z[place] = sums[...]

    @pl.loop(1, depth)
    def _(step):
        remote(sums, sums_z.at[place], qz_s, qz_r, at(line, lax.rem(place + step, depth))).start()

    back_order = [(q, a, pair) for q in range(SPLIT) for a, pair in enumerate(p.back_steps)]
    for q, _, pair in back_order:
        for k in pair:
            if k:
                to, sem = behind[k], q * depth + k
                remote(
                    half_out.at[:, :, to, :, cut(q)], land_c[q][k - 1], c_s.at[sem], c_r.at[sem], at(line, to)
                ).start()

    def back_across(q, a, pair):
        for k in pair:
            if k:
                landed(land_c[q][k - 1], c_r.at[q * depth + k])

        @pl.loop(0, lines, unroll=4)
        def _(to):
            for i, k in enumerate(pair):
                slot = tab[SLOT_ROW + lax.div(to, tall), line * depth + ahead[k]]
                if k:
                    send_d[q][a][to, i] = land_c[q][k - 1][slot, lax.rem(to, tall)]
                else:
                    send_d[q][a][to, i] = half_out[slot, lax.rem(to, tall), place, :, cut(q)]

        spot = pl.ds(p.start[a] + line * len(pair), len(pair))

        @pl.loop(1, lines, unroll=5)
        def _(step):
            to = lax.rem(line + step, lines)
            remote(
                send_d[q][a].at[to], land_d[q].at[spot],
                d_s.at[q * pairs + a], d_r.at[q * pairs + a], at(to, place),
            ).start()

        land_d[q][spot] = send_d[q][a][line]

    def back_pair(q, a, pair):
        sem = q * pairs + a
        landed(land_d[q].at[pl.ds(0, (lines - 1) * len(pair))], d_r.at[sem])
        rows = pl.ds(p.start[a], lines * len(pair))
        remote(land_d[q].at[rows], land_e[q].at[rows], y_s.at[sem], y_r.at[sem], partner).start()

    def far_landed(q):
        for a, pair in enumerate(p.back_steps):
            rows = pl.ds(p.start[a], lines * len(pair))
            landed(land_e[q].at[rows], y_r.at[q * pairs + a])

    def place_rows(q, h, source, m):
        factor = scales[pl.ds(m, 1), :]
        rows = pl.ds(pl.multiple_of(h * half, half), half)
        for c in range(columns):
            piece = source[q][tab[p.land_row + m * columns + c, 0]].astype(F32) * factor
            made[m, rows, cut(q, c)] = piece.astype(BF16)

    def place_both(q):
        far_landed(q)

        @pl.loop(0, p.matrices)
        def _(m):
            place_rows(q, core, land_d, m)
            place_rows(q, far_core, land_e, m)

    def find_scales():
        landed(sums_c.at[1], qc_r)
        total = jnp.sum(sums_c[0] + sums_c[1], axis=2, keepdims=True)
        count = float(p.slab * p.fsdp * p.model)
        scale = jnp.sqrt((total[0] / count + EPSILON) / (total[1] / count + EPSILON))
        scales[...] = jnp.broadcast_to(scale, scales.shape)

    for a in range(len(back_order) + AHEAD):
        if a < len(back_order):
            back_across(*back_order[a])
        if a == 1:
            landed(sums_z.at[pl.ds(0, depth - 1)], qz_r)
            sums_l[line] = jnp.sum(sums_z[...], axis=0)

            @pl.loop(1, lines)
            def _(step):
                remote(sums_l.at[line], sums_l.at[line], ql_s, ql_r, at(lax.rem(line + step, lines), place)).start()

        if a == pairs - 1:
            landed(sums_l.at[pl.ds(0, lines - 1)], ql_r)
            sums_c[0] = jnp.sum(sums_l[...], axis=0)
            remote(sums_c.at[0], sums_c.at[1], qc_s, qc_r, partner).start()
        if a == len(back_order):
            find_scales()
            for q in range(SPLIT - 1):
                place_both(q)
        if a >= AHEAD:
            back_pair(*back_order[a - AHEAD])

    last = SPLIT - 1

    @pl.loop(0, p.matrices)
    def _(m):
        place_rows(last, core, land_d, m)

    far_landed(last)

    @pl.loop(0, p.matrices)
    def _(m):
        place_rows(last, far_core, land_e, m)
        pltpu.make_async_copy(made.at[m], upd.at[m], save_u.at[m]).start()

    for q in range(SPLIT):
        landed(theirs.at[pl.ds(0, part_of)], pair_s.at[q])
        for a, pair in enumerate(p.out_steps):
            landed(send_a[q][a].at[pl.ds(0, lines - 1)], a_s.at[q * pairs + a])
        for a, pair in enumerate(p.back_steps):
            landed(send_d[q][a].at[pl.ds(0, lines - 1)], d_s.at[q * pairs + a])
            landed(land_d[q].at[pl.ds(p.start[a], lines * len(pair))], y_s.at[q * pairs + a])
        for k in range(depth):
            landed(blocks.at[:, :, behind[k], core, :, cut(q)], x_s.at[q * depth + k])
            if k:
                landed(send_b.at[q, k - 1], b_s.at[q * depth + k])
                landed(land_c[q][k - 1], c_s.at[q * depth + k])
    for j in range(slots):
        landed(stat.at[j], save_n.at[j])
    for i in range(share):
        landed(root.at[i], root_s.at[i])
        landed(whole.at[i, :, :, far_core], p_s.at[i])
    landed(sums_z.at[pl.ds(0, depth - 1)], qz_s)
    landed(sums_l.at[pl.ds(0, lines - 1)], ql_s)
    landed(sums_c.at[0], qc_s)
    for m in range(p.matrices):
        landed(made.at[m], save_u.at[m])


def tables(p, owner, me, line, place):
    groups, columns, lines, depth = p.groups, p.columns, p.lines, p.depth

    def bits(n):
        assert n & (n - 1) == 0
        return n.bit_length() - 1

    group = lax.shift_right_logical(owner, bits(columns)) & (groups - 1)
    matrix = lax.shift_right_logical(owner, bits(columns * groups))
    local = matrix * columns + (owner & (columns - 1))
    code = jnp.zeros((1, p.fsdp), jnp.int32)
    for j in range(p.slots):
        here = group[j : j + 1] == lax.div(me, p.span)
        code = code + jnp.where(here, local[j : j + 1] + 1, 0)
    group_id = lax.broadcasted_iota(jnp.int32, (groups, p.fsdp), 0)
    slot = jnp.zeros((groups, p.fsdp), jnp.int32)
    for j in range(1, p.slots):
        slot = slot + jnp.where(group[j : j + 1] == group_id, j, 0)
    lane = lax.broadcasted_iota(jnp.int32, (1, p.fsdp), 1)
    gap = ((lane & (depth - 1)) - place) & (depth - 1)
    land = jnp.zeros((1, p.fsdp), jnp.int32)
    for a, pair in enumerate(p.back_steps):
        for i, k in enumerate(pair):
            spot = p.start[a] + lax.shift_right_logical(lane, bits(depth)) * len(pair) + i
            land = land + jnp.where(gap == k, spot, 0)
    block_id = lax.broadcasted_iota(jnp.int32, (p.matrices * columns, p.fsdp), 0)
    hit = jnp.where(code == block_id + 1, land, 0)
    hit = jnp.broadcast_to(jnp.sum(hit, axis=1, keepdims=True), hit.shape)
    return [
        (0, jnp.clip(code - 1, 0, p.matrices * columns - 1)),
        (GROUP_ROW, group),
        (SLOT_ROW, jnp.minimum(slot, p.slots - 1)),
        (p.land_row, jnp.minimum(hit, lines * depth - 1)),
        (p.matrix_row, matrix),
    ]


def body(p, gradient, old_stats, owner_table):
    depth, lines, slots, block = p.depth, p.lines, p.slots, p.block
    half, tall, wide = p.half, p.tall, p.wide
    pairs, steps = SPLIT * p.pairs, SPLIT * depth
    dma = pltpu.SemaphoreType.DMA
    vm = pltpu.VMEM
    full = (slots, tall, depth, 2, half, block)

    def chunks(order):
        return [[vm((lines, len(pair), half, wide), BF16) for pair in order] for _ in range(SPLIT)]

    scratch = [
        vm((p.matrices, half, p.model), BF16),
        vm((p.matrices, half, p.model), BF16),
        [vm((p.matrices * p.columns, half, wide), BF16) for _ in range(SPLIT)],
        chunks(p.out_steps),
        chunks(p.out_steps),
        vm((SPLIT, depth - 1, slots, tall, half, wide), BF16),
        vm(full, BF16),
        vm((block, block), F32),
        vm(full, BF16),
        vm((2,) + full[1:], BF16),
        vm((slots, tall, depth, half, block), BF16),
        [[vm((slots, tall, half, wide), BF16) for _ in range(depth - 1)] for _ in range(SPLIT)],
        chunks(p.back_steps),
        [vm((lines * depth, half, wide), BF16) for _ in range(SPLIT)],
        vm((2, p.matrices, 128), F32),
        vm((p.matrices, wide), F32),
        vm((depth, 2, p.matrices, 128), F32),
        vm((lines, 2, p.matrices, 128), F32),
        vm((2, 2, p.matrices, 128), F32),
        vm((p.table_rows, p.fsdp), jnp.int32),
        pltpu.SMEM((p.table_rows, p.fsdp), jnp.int32),
        vm((slots, block, block), F32),
        vm((p.matrices, p.slab, p.model), BF16),
        vm((slots, p.fsdp), jnp.int32),
        vm((2,) + full[1:], BF16),
        [vm((lines * depth, half, wide), BF16) for _ in range(SPLIT)],
    ]
    counts = [SPLIT, slots, slots, p.matrices, SPLIT, SPLIT, pairs, pairs, steps, steps]
    counts += [steps, steps, 2, 2, steps, steps, pairs, pairs, pairs, pairs]
    scratch += [dma((count,)) for count in counts]
    scratch += [dma] * 8 + [dma((2,))] * 2
    update, fresh = pl.pallas_call(
        functools.partial(kernel, p),
        out_shape=(
            jax.ShapeDtypeStruct((p.matrices, p.slab, p.model), BF16),
            jax.ShapeDtypeStruct(old_stats.shape, F32),
        ),
        in_specs=[
            pl.BlockSpec(memory_space=pltpu.HBM),
            pl.BlockSpec(memory_space=pltpu.HBM),
            pl.BlockSpec(memory_space=pltpu.HBM),
        ],
        out_specs=(pl.BlockSpec(memory_space=pl.ANY), pl.BlockSpec(memory_space=pl.ANY)),
        scratch_shapes=scratch,
        compiler_params=pltpu.CompilerParams(
            collective_id=0, has_side_effects=True, vmem_limit_bytes=VMEM_BYTES
        ),
        name="shampoo",
    )(*(pltpu.with_memory_space_constraint(x, pltpu.HBM) for x in (owner_table.T, gradient, old_stats)))
    return update, fresh


def solution(mesh):
    def whole(gradient, old_stats, owner_table):
        fsdp = mesh.shape["fsdp"]
        _, matrices, rows, model = gradient.shape
        p = Plan(fsdp, matrices, rows // fsdp, model, owner_table.shape[1], old_stats.shape[2])
        return jax.shard_map(
            functools.partial(body, p),
            mesh=mesh,
            in_specs=(P("rep", None, "fsdp", None), P("rep", "fsdp", None, None), P()),
            out_specs=(P(None, "fsdp", None), P("rep", "fsdp", None, None)),
            check_vma=False,
        )(gradient, old_stats, owner_table)

    return whole
```

profile of v0, /device:TPU:1, one launch (start us, length us, event | category | flops | bytes accessed | tf_op | source)
XLA Modules:
  0.0 94.9 jit_solution(5631402682241058209)
XLA Ops:
  0.6 91.0 %shampoo.1 = (bf16[8,32,4096]{2,1,0:T(8,128)(2,1)S(1)}, f32[1,4,512,512]{3,2,1,0:T(8,128)S(1)}) custom-call(s32[4,128]{1,0:T(4,128)} %bitcast.1, bf16[1,8,32,4096]{3,2,1,0:T(8,128)(2,1)} %grad.1, f32[1,4,512,512]{3,2,1,0:T(8,128)} %old.1), custom_call_target="tpu_custom_call" | custom-call | tf_op jit(solution)/shard_map/shampoo/pallas_call | solution.py:506
  91.6 1.3 %copy.7 = bf16[8,32,4096]{2,1,0:T(8,128)(2,1)} copy(bf16[8,32,4096]{2,1,0:T(8,128)(2,1)S(1)} %get-tuple-element.4) | data formatting | bytes 4194304
  92.9 2.0 %copy.8 = f32[1,4,512,512]{3,2,1,0:T(8,128)} copy(f32[1,4,512,512]{3,2,1,0:T(8,128)S(1)} %get-tuple-element.5) | data formatting | bytes 8388608
where the time goes:
time: 95 us; the launch traced here: 94.9 us
  Pallas kernels  91 us (96%)
  local copies, waits for them, and re-layouts  3.33 us (4%)
    pallas_call x1, Pallas kernels, body(): pl.pallas_call(functools.partial(kernel, p), out_shape=(jax.ShapeDtypeStr...  91 us
    unnamed x2, local copies, waits for them, and re-layouts  3.33 us

commit v1 on v0

--- a/solution.py
+++ b/solution.py
@@ -16,7 +16,7 @@
 
 DEPTH = 8
 GROUP_ROW, SLOT_ROW = 8, 16
-AHEAD = 3
+AHEAD = 5
 SPLIT = 2
 
 COEF = tuple(
@@ -196,21 +196,26 @@
                 ).start()
 
     out_order = [(q, a, pair) for q in range(SPLIT) for a, pair in enumerate(p.out_steps)]
-    for at_step in range(len(out_order) + AHEAD):
-        if at_step % pairs == min(2, pairs - 1) and at_step // pairs + 1 < SPLIT:
-            add(at_step // pairs + 1)
-        if at_step < len(out_order):
-            across(*out_order[at_step])
-        if at_step >= AHEAD:
-            along(*out_order[at_step - AHEAD])
-
-    for q, _, pair in out_order:
+
+    def pair_up(q, _, pair):
         for k in pair:
             rows = blocks.at[:, :, behind[k], core, :, cut(q)]
             sem = q * depth + k
             if k:
                 landed(rows, b_r.at[sem])
             remote(rows, rows, x_s.at[sem], x_r.at[sem], partner).start()
+
+    late = AHEAD + 3
+    for at_step in range(len(out_order) + late):
+        if at_step % pairs == min(2, pairs - 1) and at_step // pairs + 1 < SPLIT:
+            add(at_step // pairs + 1)
+        if at_step < len(out_order):
+            across(*out_order[at_step])
+        if AHEAD <= at_step < len(out_order) + AHEAD:
+            along(*out_order[at_step - AHEAD])
+        if at_step >= late:
+            pair_up(*out_order[at_step - late])
+
     for q, _, pair in out_order:
         for k in pair:
             landed(blocks.at[:, :, behind[k], far_core, :, cut(q)], x_r.at[q * depth + k])

time: 95 us -> 95.5 us (level)
  no operation moved by 1% of the time
where the time goes in v1:
time: 95.5 us; the launch traced here: 95.4 us
  Pallas kernels  91.4 us (96%)
  local copies, waits for them, and re-layouts  3.33 us (3%)
    pallas_call x1, Pallas kernels, body(): pl.pallas_call(functools.partial(kernel, p), out_shape=(jax.ShapeDtypeStr...  91.4 us
    unnamed x2, local copies, waits for them, and re-layouts  3.33 us

profile of v1, /device:TPU:1, one launch (start us, length us, event | category | flops | bytes accessed | tf_op | source)
XLA Modules:
  0.0 95.4 jit_solution(6030864808657481733)
XLA Ops:
  0.6 91.4 %shampoo.1 = (bf16[8,32,4096]{2,1,0:T(8,128)(2,1)S(1)}, f32[1,4,512,512]{3,2,1,0:T(8,128)S(1)}) custom-call(s32[4,128]{1,0:T(4,128)} %bitcast.1, bf16[1,8,32,4096]{3,2,1,0:T(8,128)(2,1)} %grad.1, f32[1,4,512,512]{3,2,1,0:T(8,128)} %old.1), custom_call_target="tpu_custom_call" | custom-call | tf_op jit(solution)/shard_map/shampoo/pallas_call | solution.py:511
  92.0 1.3 %copy.7 = bf16[8,32,4096]{2,1,0:T(8,128)(2,1)} copy(bf16[8,32,4096]{2,1,0:T(8,128)(2,1)S(1)} %get-tuple-element.4) | data formatting | bytes 4194304
  93.4 2.0 %copy.8 = f32[1,4,512,512]{3,2,1,0:T(8,128)} copy(f32[1,4,512,512]{3,2,1,0:T(8,128)S(1)} %get-tuple-element.5) | data formatting | bytes 8388608

commit v2 on v0

--- a/solution.py
+++ b/solution.py
@@ -379,7 +379,7 @@
             landed(sums_l.at[pl.ds(0, lines - 1)], ql_r)
             sums_c[0] = jnp.sum(sums_l[...], axis=0)
             remote(sums_c.at[0], sums_c.at[1], qc_s, qc_r, partner).start()
-        if a == len(back_order):
+        if a == len(back_order) + AHEAD - 1:
             find_scales()
             for q in range(SPLIT - 1):
                 place_both(q)

time: 95 us -> 95 us (level)
  no operation moved by 1% of the time
where the time goes in v2:
time: 95 us; the launch traced here: 94.9 us
  Pallas kernels  91 us (96%)
  local copies, waits for them, and re-layouts  3.33 us (4%)
    pallas_call x1, Pallas kernels, body(): pl.pallas_call(functools.partial(kernel, p), out_shape=(jax.ShapeDtypeStr...  91 us
    unnamed x2, local copies, waits for them, and re-layouts  3.33 us

profile of v2, /device:TPU:1, one launch (start us, length us, event | category | flops | bytes accessed | tf_op | source)
XLA Modules:
  0.0 94.9 jit_solution(8670425668317997367)
XLA Ops:
  0.6 91.0 %shampoo.1 = (bf16[8,32,4096]{2,1,0:T(8,128)(2,1)S(1)}, f32[1,4,512,512]{3,2,1,0:T(8,128)S(1)}) custom-call(s32[4,128]{1,0:T(4,128)} %bitcast.1, bf16[1,8,32,4096]{3,2,1,0:T(8,128)(2,1)} %grad.1, f32[1,4,512,512]{3,2,1,0:T(8,128)} %old.1), custom_call_target="tpu_custom_call" | custom-call | tf_op jit(solution)/shard_map/shampoo/pallas_call | solution.py:506
  91.6 1.3 %copy.7 = bf16[8,32,4096]{2,1,0:T(8,128)(2,1)} copy(bf16[8,32,4096]{2,1,0:T(8,128)(2,1)S(1)} %get-tuple-element.4) | data formatting | bytes 4194304
  92.9 2.0 %copy.8 = f32[1,4,512,512]{3,2,1,0:T(8,128)} copy(f32[1,4,512,512]{3,2,1,0:T(8,128)S(1)} %get-tuple-element.5) | data formatting | bytes 8388608
